TPU v7x, 512 devices: a whole 4x8x8 slice. The times are simulated.
512 devices in a mesh: section: 4 (over x), ctx: 128 (over y, z, core).
Axes of the slice: x: 4, y: 8, z: 8, core: 2. Of those that a mesh axis runs over, the one named last changes fastest.
Arguments:
- query_in: bfloat16 [4, 2, 16384, 2048], P('section', None, 'ctx'), may hold values from -24 to 24
- key_in: bfloat16 [4, 2, 16384, 256], P('section', None, 'ctx'), may hold values from -24 to 24
- value_in: bfloat16 [4, 2, 16384, 256], P('section', None, 'ctx'), may hold values from -5 to 5
- doc_ids: int32 [2, 16384], replicated, may hold values from 0 to 159, never falling along the last dimension, each value on 1 to 128 neighbouring positions
- out_grad: bfloat16 [2, 16384, 2048], P(None, 'ctx'), may hold values from -5 to 5
Outputs:
- attention: bfloat16 [4, 2, 16384, 2048], P('section', None, 'ctx')
- query_grad: bfloat16 [4, 2, 16384, 2048], P('section', None, 'ctx')
- key_grad: bfloat16 [4, 2, 16384, 256], P('section', None, 'ctx')
- value_grad: bfloat16 [4, 2, 16384, 256], P('section', None, 'ctx')
Inputs may be any that keep to these rules, and one draw needn't show every extreme that they name: `doc_ids`: never falling along the tokens; each document holds 1 to 128 tokens, one exactly 128.
All inputs are finite; a program needn't handle non-finite values.
Results may differ from a plain program's by a relative error of at most 0.012.
The roundings to bfloat16 on the way count: a program that leaves them out, or rounds other values in their place, can miss the bound.
Values may be sent and summed in bfloat16 or wider, within the bound.
A program may use at most 128 MiB of HBM per device.

v0:
```python
import functools
import math

import jax
import jax.numpy as jnp
from jax import lax
from jax.experimental import pallas as pl
from jax.experimental.pallas import tpu as pltpu
from jax.sharding import PartitionSpec as P

HD = 128
GROUP = 8
KVH = 2
HEADS = GROUP * KVH
MB = 2
TOK = 128
G = 1
CPG = GROUP // G
NGRP = MB * KVH
NCH = NGRP * CPG
ROWS = G * TOK
DELAY = 3
MESH = pl.DeviceIdType.MESH
SCALE = 1.0 / math.sqrt(HD)
EXP2_SCALE = math.log2(math.e) / math.sqrt(HD)
NT = (((1,), (1,)), ((), ()))
NN = (((1,), (0,)), ((), ()))
TN = (((0,), (0,)), ((), ()))


def dot(a, b, dims):
    return lax.dot_general(a, b, dims, preferred_element_type=jnp.float32)


def kernel(
    sections,
    shards_n,
    q_hbm,
    k_hbm,
    v_hbm,
    ids_hbm,
    og_hbm,
    att_hbm,
    qg_hbm,
    kg_hbm,
    vg_hbm,
    qbuf,
    frecv,
    mixbuf,
    wbuf,
    pbuf,
    obuf,
    brecv,
    dqbuf,
    kcat,
    vcat,
    bias,
    own_ids,
    prev_ids,
    dkt,
    dvt,
    part_send,
    part_recv,
    kgbuf,
    vgbuf,
    q_sem,
    kv_sem,
    ids_sem,
    halo_send,
    halo_recv,
    f_send,
    f_recv,
    b_send,
    b_recv,
    part_send_sem,
    part_recv_sem,
    out_sem,
    kvout_sem,
):
    s = lax.axis_index("section")
    c = lax.axis_index("ctx")
    last = sections - 1
    first_shard = c == 0
    last_shard = c == shards_n - 1

    barrier = pltpu.get_barrier_semaphore()
    for peer in (
        (lax.rem(s + 1, sections), c),
        (lax.rem(s + sections - 1, sections), c),
        (s, lax.rem(c + 1, shards_n)),
        (s, lax.rem(c + shards_n - 1, shards_n)),
    ):
        pl.semaphore_signal(barrier, inc=1, device_id=peer, device_id_type=MESH)

    own_at = pl.multiple_of(c * TOK, TOK)
    prev_at = pl.multiple_of(jnp.maximum(c - 1, 0) * TOK, TOK)
    own_copy = pltpu.make_async_copy(ids_hbm.at[:, pl.ds(own_at, TOK)], own_ids, ids_sem.at[0])
    prev_copy = pltpu.make_async_copy(ids_hbm.at[:, pl.ds(prev_at, TOK)], prev_ids, ids_sem.at[1])
    own_copy.start()
    prev_copy.start()

    def head_cols(ref, chunk, head):
        m = chunk // (KVH * CPG)
        col = lax.rem(chunk, KVH * CPG) * G + head
        return ref.at[m, :, pl.ds(pl.multiple_of(col * HD, HD), HD)]

    def head_rows(ref, chunk, head):
        return ref.at[chunk, pl.ds(head * TOK, TOK)]

    for grp in range(NGRP):
        m, n = divmod(grp, KVH)
        for which, (src, dst) in enumerate(((k_hbm, kcat), (v_hbm, vcat))):
            pltpu.make_async_copy(
                src.at[m, :, pl.ds(n * HD, HD)], dst.at[grp, pl.ds(TOK, TOK)], kv_sem.at[which]
            ).start()

    @pl.loop(0, NCH)
    def _(i):
        for head in range(G):
            pltpu.make_async_copy(head_cols(q_hbm, i, head), head_rows(qbuf, i, head), q_sem).start()

    @pl.when(s == last)
    def _():
        @pl.loop(0, NCH)
        def _(i):
            for head in range(G):
                pltpu.make_async_copy(
                    head_cols(og_hbm, i, head), head_rows(brecv, i, head), b_recv.at[i]
                ).start()

    dkt[...] = jnp.zeros_like(dkt)
    dvt[...] = jnp.zeros_like(dvt)

    @pl.when(s == 0)
    def _():
        frecv[...] = jnp.zeros_like(frecv)

    @pl.when(first_shard)
    def _():
        for grp in range(NGRP):
            kcat[grp, :TOK] = jnp.zeros((TOK, HD), jnp.bfloat16)
            vcat[grp, :TOK] = jnp.zeros((TOK, HD), jnp.bfloat16)

    pl.semaphore_wait(barrier, 4)

    def halo(grp, which):
        m, n = divmod(grp, KVH)
        src, dst = ((k_hbm, kcat), (v_hbm, vcat))[which]
        return pltpu.make_async_remote_copy(
            src_ref=src.at[m, :, pl.ds(n * HD, HD)],
            dst_ref=dst.at[grp, pl.ds(0, TOK)],
            send_sem=halo_send.at[2 * grp + which],
            recv_sem=halo_recv.at[2 * grp + which],
            device_id=(s, jnp.minimum(c + 1, shards_n - 1)),
            device_id_type=MESH,
        )

    @pl.when(jnp.logical_not(last_shard))
    def _():
        for grp in range(NGRP):
            for which in range(2):
                halo(grp, which).start()

    row = lax.broadcasted_iota(jnp.int32, (TOK, TOK), 0)
    col = lax.broadcasted_iota(jnp.int32, (TOK, TOK), 1)
    own_copy.wait()
    prev_copy.wait()
    for m in range(MB):
        own_row = jnp.broadcast_to(own_ids[m : m + 1, :], (TOK, TOK)).astype(jnp.float32)
        prev_row = jnp.broadcast_to(prev_ids[m : m + 1, :], (TOK, TOK)).astype(jnp.float32)
        prev_row = jnp.where(first_shard, -1.0, prev_row)
        seen = jnp.where(col <= row, own_row, prev_row)
        bias[m] = jnp.where(seen == own_row.T, 0.0, -1e30)
    pltpu.make_async_copy(qbuf, qbuf, q_sem).wait()
    for which, dst in enumerate((kcat, vcat)):
        view = dst.at[:, pl.ds(TOK, TOK)]
        pltpu.make_async_copy(view, view, kv_sem.at[which]).wait()

    def tri():
        rows = lax.broadcasted_iota(jnp.int32, (ROWS, TOK), 0)
        cols = lax.broadcasted_iota(jnp.int32, (ROWS, TOK), 1)
        return cols <= lax.rem(rows, TOK)

    def split(weights):
        own = tri()
        prev_half = jnp.where(own, 0.0, weights).astype(jnp.bfloat16)
        own_half = jnp.where(own, weights, 0.0).astype(jnp.bfloat16)
        return jnp.concatenate([prev_half, own_half], axis=1)

    def merge(wide):
        return jnp.where(tri(), wide[:, TOK:], wide[:, :TOK])

    def f_copy(i):
        return pltpu.make_async_remote_copy(
            src_ref=obuf.at[i],
            dst_ref=frecv.at[i],
            send_sem=f_send,
            recv_sem=f_recv.at[i],
            device_id=(jnp.minimum(s + 1, last), c),
            device_id_type=MESH,
        )

    def b_copy(i):
        return pltpu.make_async_remote_copy(
            src_ref=dqbuf.at[i],
            dst_ref=brecv.at[i],
            send_sem=b_send,
            recv_sem=b_recv.at[i],
            device_id=(jnp.maximum(s - 1, 0), c),
            device_id_type=MESH,
        )

    def part_copy(grp):
        return pltpu.make_async_remote_copy(
            src_ref=part_send.at[grp],
            dst_ref=part_recv.at[grp],
            send_sem=part_send_sem,
            recv_sem=part_recv_sem.at[grp],
            device_id=(s, jnp.maximum(c - 1, 0)),
            device_id_type=MESH,
        )

    def wait_forward(i):
        grp = i // CPG

        @pl.when(jnp.logical_and(lax.rem(i, CPG) == 0, jnp.logical_not(first_shard)))
        def _():
            for which, dst in enumerate((kcat, vcat)):
                view = dst.at[grp, pl.ds(0, TOK)]
                pltpu.make_async_copy(view, view, halo_recv.at[2 * grp + which]).wait()

        @pl.when(s > 0)
        def _():
            pltpu.make_async_copy(frecv.at[i], frecv.at[i], f_recv.at[i]).wait()

    def wait_backward(i):
        pltpu.make_async_copy(brecv.at[i], brecv.at[i], b_recv.at[i]).wait()

    def forward(i):
        grp = i // CPG
        mixed = (qbuf[i].astype(jnp.float32) + frecv[i].astype(jnp.float32)).astype(jnp.bfloat16)
        scores = merge(dot(mixed, kcat[grp], NT))
        mask = bias[grp // KVH]
        scores = scores + (mask if G == 1 else jnp.concatenate([mask] * G, axis=0))
        lifted = jnp.exp2((scores - jnp.max(scores, axis=1, keepdims=True)) * EXP2_SCALE)
        weights = lifted * (1.0 / jnp.sum(lifted, axis=1, keepdims=True))
        wide = split(weights)
        out = dot(wide, vcat[grp], NN).astype(jnp.bfloat16)
        return mixed, weights, wide, out

    def store_forward(i, results):
        mixbuf[i], wbuf[i], pbuf[i], obuf[i] = results

    def send_forward(i):
        @pl.when(s < last)
        def _():
            f_copy(i).start()

        for head in range(G):
            pltpu.make_async_copy(head_rows(obuf, i, head), head_cols(att_hbm, i, head), out_sem.at[0]).start()

    def backward(i):
        grp = i // CPG
        grad = brecv[i]
        weights = wbuf[i]
        weight_grad = merge(dot(grad, vcat[grp], NT))
        row_dot = jnp.sum(weights * weight_grad, axis=1, keepdims=True)
        wide = split(weights * (weight_grad - row_dot) * SCALE)
        return wide, dot(wide, kcat[grp], NN).astype(jnp.bfloat16)

    def kv_terms(i, wide, mixed, probs):
        return dot(mixed, wide, TN), dot(brecv[i], probs, TN)

    def send_backward(i):
        @pl.when(s > 0)
        def _():
            b_copy(i).start()

        for head in range(G):
            pltpu.make_async_copy(head_rows(dqbuf, i, head), head_cols(qg_hbm, i, head), out_sem.at[1]).start()

    def finish_group(i):
        grp = i // CPG

        @pl.when(lax.rem(i, CPG) == CPG - 1)
        def _():
            @pl.when(jnp.logical_not(first_shard))
            def _():
                part_send[grp, 0] = dkt[grp, :, :TOK].astype(jnp.bfloat16)
                part_send[grp, 1] = dvt[grp, :, :TOK].astype(jnp.bfloat16)
                part_copy(grp).start()

    warm = 2 * DELAY * (last - s) + 1

    @pl.loop(0, warm)
    def _(t):
        wait_forward(t)
        store_forward(t, forward(t))
        send_forward(t)

    @pl.loop(warm, NCH)
    def _(t):
        b = t - warm
        wait_forward(t)
        wait_backward(b)
        grp = b // CPG
        mixed, probs = mixbuf[b], pbuf[b]
        wide, grad_out = backward(b)
        dqbuf[b] = grad_out
        dk, dv = kv_terms(b, wide, mixed, probs)
        dkt[grp] += dk
        dvt[grp] += dv
        store_forward(t, forward(t))
        send_forward(t)
        send_backward(b)
        finish_group(b)

    @pl.loop(NCH, NCH + warm)
    def _(t):
        b = t - warm
        wait_backward(b)
        grp = b // CPG
        wide, grad_out = backward(b)
        dqbuf[b] = grad_out
        send_backward(b)
        dk, dv = kv_terms(b, wide, mixbuf[b], pbuf[b])
        dkt[grp] += dk
        dvt[grp] += dv
        finish_group(b)

    for grp in range(NGRP):
        m, n = divmod(grp, KVH)

        @pl.when(jnp.logical_not(last_shard))
        def _():
            pltpu.make_async_copy(part_recv.at[grp], part_recv.at[grp], part_recv_sem.at[grp]).wait()

        for which, (acc, dst) in enumerate(((dkt, kgbuf), (dvt, vgbuf))):
            extra = jnp.where(last_shard, 0.0, part_recv[grp, which].astype(jnp.float32))
            dst[m, :, n * HD : (n + 1) * HD] = (acc[grp, :, TOK:] + extra).T.astype(jnp.bfloat16)
    kv_out = (
        pltpu.make_async_copy(kgbuf, kg_hbm, kvout_sem.at[0]),
        pltpu.make_async_copy(vgbuf, vg_hbm, kvout_sem.at[1]),
    )
    for copy in kv_out:
        copy.start()

    @pl.when(jnp.logical_not(last_shard))
    def _():
        for grp in range(NGRP):
            for which in range(2):
                halo(grp, which).wait_send()

    @pl.when(jnp.logical_not(first_shard))
    def _():
        pltpu.make_async_copy(part_send, part_send, part_send_sem).wait()

    @pl.when(s < last)
    def _():
        pltpu.make_async_copy(obuf, obuf, f_send).wait()

    @pl.when(s > 0)
    def _():
        pltpu.make_async_copy(dqbuf, dqbuf, b_send).wait()

    pltpu.make_async_copy(obuf, obuf, out_sem.at[0]).wait()
    pltpu.make_async_copy(dqbuf, dqbuf, out_sem.at[1]).wait()
    for copy in kv_out:
        copy.wait()


def shards(query_in, key_in, value_in, doc_ids, out_grad):
    sections = lax.axis_size("section")
    shards_n = lax.axis_size("ctx")
    bf16, f32 = jnp.bfloat16, jnp.float32
    feat, kv = HEADS * HD, KVH * HD
    hbm = pl.BlockSpec(memory_space=pl.ANY)
    dma = pltpu.SemaphoreType.DMA
    att, qg, kg, vg = pl.pallas_call(
        functools.partial(kernel, sections, shards_n),
        out_shape=(
            jax.ShapeDtypeStruct((MB, TOK, feat), bf16),
            jax.ShapeDtypeStruct((MB, TOK, feat), bf16),
            jax.ShapeDtypeStruct((MB, TOK, kv), bf16),
            jax.ShapeDtypeStruct((MB, TOK, kv), bf16),
        ),
        in_specs=[hbm] * 5,
        out_specs=[hbm] * 4,
        scratch_shapes=[
            pltpu.VMEM((NCH, ROWS, HD), bf16),
            pltpu.VMEM((NCH, ROWS, HD), bf16),
            pltpu.VMEM((NCH, ROWS, HD), bf16),
            pltpu.VMEM((NCH, ROWS, TOK), f32),
            pltpu.VMEM((NCH, ROWS, 2 * TOK), bf16),
            pltpu.VMEM((NCH, ROWS, HD), bf16),
            pltpu.VMEM((NCH, ROWS, HD), bf16),
            pltpu.VMEM((NCH, ROWS, HD), bf16),
            pltpu.VMEM((NGRP, 2 * TOK, HD), bf16),
            pltpu.VMEM((NGRP, 2 * TOK, HD), bf16),
            pltpu.VMEM((MB, TOK, TOK), f32),
            pltpu.VMEM((MB, TOK), jnp.int32),
            pltpu.VMEM((MB, TOK), jnp.int32),
            pltpu.VMEM((NGRP, HD, 2 * TOK), f32),
            pltpu.VMEM((NGRP, HD, 2 * TOK), f32),
            pltpu.VMEM((NGRP, 2, HD, TOK), bf16),
            pltpu.VMEM((NGRP, 2, HD, TOK), bf16),
            pltpu.VMEM((MB, TOK, kv), bf16),
            pltpu.VMEM((MB, TOK, kv), bf16),
            dma,
            dma((2,)),
            dma((2,)),
            dma((2 * NGRP,)),
            dma((2 * NGRP,)),
            dma,
            dma((NCH,)),
            dma,
            dma((NCH,)),
            dma,
            dma((NGRP,)),
            dma((2,)),
            dma((2,)),
        ],
        compiler_params=pltpu.CompilerParams(
            collective_id=0, has_side_effects=True, vmem_limit_bytes=40 * 1024 * 1024
        ),
        cost_estimate=pl.CostEstimate(flops=2_000_000_000, bytes_accessed=5_000_000, transcendentals=600_000),
    )(query_in[0], key_in[0], value_in[0], doc_ids, out_grad)
    return (att[None], qg[None], kg[None], vg[None])


def solution(mesh):
    split = P("section", None, "ctx", None)
    return jax.shard_map(
        shards,
        mesh=mesh,
        in_specs=(split, split, split, P(), P(None, "ctx", None)),
        out_specs=(split, split, split, split),
        check_vma=False,
    )
```

profile of v0, /device:TPU:56, one launch (start us, length us, event | category | flops | bytes accessed | tf_op | source)
XLA Modules:
  0.0 86.5 jit_solution(7458043637927394636)
XLA Ops:
  0.6 0.0 copy-start
  0.6 1.2 %copy-done = bf16[1,2,128,2048]{3,2,1,0:T(8,128)(2,1)S(1)} copy-done((bf16[1,2,128,2048]{3,2,1,0:T(8,128)(2,1)S(1)}, bf16[1,2,128,2048]{3,2,1,0:T(8,128)(2,1)}, u32[]{:S(2)}) %copy-start) | copy-done | bytes 1048600
  1.9 0.0 copy-start.1
  1.9 1.2 %copy-done.1 = bf16[2,128,2048]{2,1,0:T(8,128)(2,1)S(1)} copy-done((bf16[2,128,2048]{2,1,0:T(8,128)(2,1)S(1)}, bf16[2,128,2048]{2,1,0:T(8,128)(2,1)}, u32[]{:S(2)}) %copy-start.1) | copy-done | bytes 1048600
  3.1 0.0 copy-start.2
  3.1 0.9 %copy-done.2 = bf16[1,2,128,256]{3,2,1,0:T(8,128)(2,1)S(1)} copy-done((bf16[1,2,128,256]{3,2,1,0:T(8,128)(2,1)S(1)}, bf16[1,2,128,256]{3,2,1,0:T(8,128)(2,1)}, u32[]{:S(2)}) %copy-start.2) | copy-done | bytes 131096
  4.0 0.0 copy-start.3
  4.0 0.9 %copy-done.3 = bf16[1,2,128,256]{3,2,1,0:T(8,128)(2,1)S(1)} copy-done((bf16[1,2,128,256]{3,2,1,0:T(8,128)(2,1)S(1)}, bf16[1,2,128,256]{3,2,1,0:T(8,128)(2,1)}, u32[]{:S(2)}) %copy-start.3) | copy-done | bytes 131096
  4.9 0.0 copy-start.4
  4.9 0.9 %copy-done.4 = s32[2,16384]{1,0:T(2,128)S(1)} copy-done((s32[2,16384]{1,0:T(2,128)S(1)}, s32[2,16384]{1,0:T(2,128)}, u32[]{:S(2)}) %copy-start.4) | copy-done | bytes 131096
  5.8 77.5 %shard_map.84 = (bf16[2,128,2048]{2,1,0:T(8,128)(2,1)S(1)}, bf16[2,128,2048]{2,1,0:T(8,128)(2,1)S(1)}, bf16[2,128,256]{2,1,0:T(8,128)(2,1)S(1)}, bf16[2,128,256]{2,1,0:T(8,128)(2,1)S(1)}) custom-call(bf16[2,128,2048]{2,1,0:T(8,128)(2,1)S(1)} %bitcast.11, bf16[2,128,256]{2,1,0:T(8,128)(2,1)S(1)} %bitcast.12, bf16[2,128,256]{2,1,0:T(8,128)(2,1)S(1)} %bitcast.13, ...), custom_call_target="tpu_custom_call" | custom-call | flops 2000000000 | bytes 5000000 | tf_op jit(solution)/shard_map/pallas_call | solution.py:379
  83.3 1.0 %copy.13 = bf16[1,2,128,2048]{3,2,1,0:T(8,128)(2,1)} copy(bf16[1,2,128,2048]{3,2,1,0:T(8,128)(2,1)S(1)} %bitcast.8) | data formatting | bytes 2097152
  84.3 1.0 %copy.14 = bf16[1,2,128,2048]{3,2,1,0:T(8,128)(2,1)} copy(bf16[1,2,128,2048]{3,2,1,0:T(8,128)(2,1)S(1)} %bitcast.7) | data formatting | bytes 2097152
  85.2 0.7 copy.15
  85.9 0.7 copy.16
Async XLA Ops:
  0.6 1.2 %copy-start = (bf16[1,2,128,2048]{3,2,1,0:T(8,128)(2,1)S(1)}, bf16[1,2,128,2048]{3,2,1,0:T(8,128)(2,1)}, u32[]{:S(2)}) copy-start(bf16[1,2,128,2048]{3,2,1,0:T(8,128)(2,1)} %param.5) | copy-start | bytes 3145732
  1.9 1.2 %copy-start.1 = (bf16[2,128,2048]{2,1,0:T(8,128)(2,1)S(1)}, bf16[2,128,2048]{2,1,0:T(8,128)(2,1)}, u32[]{:S(2)}) copy-start(bf16[2,128,2048]{2,1,0:T(8,128)(2,1)} %og_hbm.1) | copy-start | bytes 3145732
  3.1 0.9 %copy-start.2 = (bf16[1,2,128,256]{3,2,1,0:T(8,128)(2,1)S(1)}, bf16[1,2,128,256]{3,2,1,0:T(8,128)(2,1)}, u32[]{:S(2)}) copy-start(bf16[1,2,128,256]{3,2,1,0:T(8,128)(2,1)} %param.6) | copy-start | bytes 393220
  4.0 0.9 %copy-start.3 = (bf16[1,2,128,256]{3,2,1,0:T(8,128)(2,1)S(1)}, bf16[1,2,128,256]{3,2,1,0:T(8,128)(2,1)}, u32[]{:S(2)}) copy-start(bf16[1,2,128,256]{3,2,1,0:T(8,128)(2,1)} %param.7) | copy-start | bytes 393220
  4.9 0.9 %copy-start.4 = (s32[2,16384]{1,0:T(2,128)S(1)}, s32[2,16384]{1,0:T(2,128)}, u32[]{:S(2)}) copy-start(s32[2,16384]{1,0:T(2,128)} %ids_hbm.1) | copy-start | bytes 393220
where the time goes:
time: 86.8 us; the launch traced here: 86.5 us
  Pallas kernels  77.5 us (89%)
  local copies, waits for them, and re-layouts  8.4 us (10%)
    pallas_call x1, Pallas kernels, shards(): pl.pallas_call(functools.partial(kernel, sections, shards_n), out_shape=(...  77.5 us
    unnamed x14, local copies, waits for them, and re-layouts  8.4 us

commit v1 on v0

v1 whole, which is shorter than its diff:
```python
import functools
import math

import jax
import jax.numpy as jnp
from jax import lax
from jax.experimental import pallas as pl
from jax.experimental.pallas import tpu as pltpu
from jax.sharding import PartitionSpec as P

HD = 128
GROUP = 8
KVH = 2
HEADS = GROUP * KVH
MB = 2
TOK = 128
LAYERS = 4
NGRP = MB * KVH
G = 4
NU = GROUP // G
COLS = G * HD
ROWS = G * TOK
SLOTS = 4
MESH = pl.DeviceIdType.MESH
SCALE = 1.0 / math.sqrt(HD)
EXP2_SCALE = math.log2(math.e) / math.sqrt(HD)
NT = (((1,), (1,)), ((), ()))
NN = (((1,), (0,)), ((), ()))
TN = (((0,), (0,)), ((), ()))

PLACE = (
    (0, 0, 0, 0),
    (1, 1, 1, 1),
    (2, 2, 2, 2),
    (3, 3, 3, 3),
)
ORDER = (
    (0, 1, 4, 8, 12, 28, 24, 20, 5, 16, 9, 13, 29, 25, 21, 17),
    (0, 4, 8, 12, 28, 24, 20, 16, 1, 5, 9, 13, 29, 25, 21, 17),
    (0, 4, 8, 12, 28, 24, 20, 16, 1, 5, 9, 13, 29, 25, 21, 17),
    (0, 4, 8, 12, 28, 24, 20, 16, 1, 5, 9, 13, 29, 25, 21, 17),
)
PAIRS = tuple(
    tuple((g, l) for g in range(NGRP) for l in range(LAYERS) if PLACE[g][l] == x) for x in range(LAYERS)
)
SLOT = tuple(tuple(PAIRS[PLACE[g][l]].index((g, l)) for l in range(LAYERS)) for g in range(NGRP))
STEPS = 2 * SLOTS * NU
PER_WORD = 6


def packed(numbers):
    return tuple(
        sum(n << (5 * j) for j, n in enumerate(numbers[i : i + PER_WORD])) for i in range(0, STEPS, PER_WORD)
    )


def pair_code(g, l):
    after, before = min(l + 1, LAYERS - 1), max(l - 1, 0)
    fields = (g, l, PLACE[g][after], SLOT[g][after], PLACE[g][before], SLOT[g][before])
    return sum(n << (2 * j) for j, n in enumerate(fields))


def choose(index, values):
    out = values[-1]
    for j in range(len(values) - 2, -1, -1):
        if not (isinstance(out, int) and isinstance(values[j], int) and out == values[j]):
            out = jnp.where(index == j, values[j], out)
    return out


def field(code, j):
    return lax.rem(lax.shift_right_logical(code, jnp.int32(2 * j)), 4)


def dot(a, b, dims):
    return lax.dot_general(a, b, dims, preferred_element_type=jnp.float32)


def stack_heads(x):
    return jnp.concatenate([x[:, h * HD : (h + 1) * HD] for h in range(G)], axis=0)


def side_by_side(x):
    return jnp.concatenate([x[h * TOK : (h + 1) * TOK] for h in range(G)], axis=1)


def kernel(
    shards_n,
    q_hbm,
    k_hbm,
    v_hbm,
    ids_hbm,
    og_hbm,
    att_hbm,
    qg_hbm,
    kg_hbm,
    vg_hbm,
    qbuf,
    fin,
    gin,
    obuf,
    dqbuf,
    mixbuf,
    wbuf,
    pbuf,
    kcat,
    vcat,
    bias,
    own_ids,
    prev_ids,
    dkt,
    dvt,
    part_send,
    part_recv,
    kvout,
    ids_sem,
    q_send,
    q_recv,
    kv_send,
    kv_recv,
    halo_send,
    halo_recv,
    f_send,
    f_recv,
    b_send,
    b_recv,
    part_send_sem,
    part_recv_sem,
    home_send,
    home_recv,
):
    x = lax.axis_index("section")
    c = lax.axis_index("ctx")
    first_shard = c == 0
    last_shard = c == shards_n - 1

    barrier = pltpu.get_barrier_semaphore()
    for d in range(1, LAYERS):
        pl.semaphore_signal(barrier, inc=1, device_id=(lax.rem(x + d, LAYERS), c), device_id_type=MESH)

    @pl.when(jnp.logical_not(first_shard))
    def _():
        pl.semaphore_signal(barrier, inc=1, device_id=(x, jnp.maximum(c - 1, 0)), device_id_type=MESH)

    codes = [choose(x, [pair_code(*PAIRS[s][slot]) for s in range(LAYERS)]) for slot in range(SLOTS)]
    words = [
        choose(x, [packed(ORDER[s])[w] for s in range(LAYERS)]) for w in range((STEPS + PER_WORD - 1) // PER_WORD)
    ]

    def move(src, dst, send_sem, recv_sem, section):
        return pltpu.make_async_remote_copy(
            src_ref=src,
            dst_ref=dst,
            send_sem=send_sem,
            recv_sem=recv_sem,
            device_id=(section, c),
            device_id_type=MESH,
        )

    def wait_for(ref, sem):
        pltpu.make_async_copy(ref, ref, sem).wait()

    def columns(ref, group, unit):
        m, n = group // KVH, lax.rem(group, KVH)
        return ref.at[m, :, pl.ds(pl.multiple_of(n * GROUP * HD + unit * COLS, COLS), COLS)]

    def kv_columns(ref, group):
        m, n = group // KVH, lax.rem(group, KVH)
        return ref.at[m, :, pl.ds(pl.multiple_of(n * HD, HD), HD)]

    places = [(choose(x, PLACE[g]), choose(x, SLOT[g])) for g in range(NGRP)]

    own_at = pl.multiple_of(c * TOK, TOK)
    prev_at = pl.multiple_of(jnp.maximum(c - 1, 0) * TOK, TOK)
    own_copy = pltpu.make_async_copy(ids_hbm.at[:, pl.ds(own_at, TOK)], own_ids, ids_sem.at[0])
    prev_copy = pltpu.make_async_copy(ids_hbm.at[:, pl.ds(prev_at, TOK)], prev_ids, ids_sem.at[1])
    own_copy.start()
    prev_copy.start()

    for g, (section, slot) in enumerate(places):

        @pl.when(section == x)
        def _():
            for which, (src, dst) in enumerate(((k_hbm, kcat), (v_hbm, vcat))):
                pltpu.make_async_copy(
                    kv_columns(src, g), dst.at[slot, pl.ds(TOK, TOK)], kv_recv.at[2 * slot + which]
                ).start()
            for u in range(NU):
                pltpu.make_async_copy(columns(q_hbm, g, u), qbuf.at[slot, u], q_recv.at[slot * NU + u]).start()

    for slot in range(SLOTS):

        @pl.when(field(codes[slot], 1) == LAYERS - 1)
        def _():
            for u in range(NU):
                pltpu.make_async_copy(
                    columns(og_hbm, field(codes[slot], 0), u), gin.at[slot, u], b_recv.at[slot * NU + u]
                ).start()

    dkt[...] = jnp.zeros_like(dkt)
    dvt[...] = jnp.zeros_like(dvt)

    @pl.when(first_shard)
    def _():
        for slot in range(SLOTS):
            kcat[slot, :TOK] = jnp.zeros((TOK, HD), jnp.bfloat16)
            vcat[slot, :TOK] = jnp.zeros((TOK, HD), jnp.bfloat16)

    pl.semaphore_wait(barrier, jnp.where(last_shard, LAYERS - 1, LAYERS))

    def kv_move(g, which):
        section, slot = places[g]
        src, dst = ((k_hbm, kcat), (v_hbm, vcat))[which]
        return move(
            kv_columns(src, g),
            dst.at[slot, pl.ds(TOK, TOK)],
            kv_send.at[2 * g + which],
            kv_recv.at[2 * slot + which],
            section,
        )

    def q_move(g, u):
        section, slot = places[g]
        return move(
            columns(q_hbm, g, u), qbuf.at[slot, u], q_send.at[g * NU + u], q_recv.at[slot * NU + u], section
        )

    for g in range(NGRP):

        @pl.when(places[g][0] != x)
        def _():
            for which in range(2):
                kv_move(g, which).start()

    for u in range(NU):
        for g in range(NGRP):

            @pl.when(places[g][0] != x)
            def _():
                q_move(g, u).start()

    row = lax.broadcasted_iota(jnp.int32, (TOK, TOK), 0)
    col = lax.broadcasted_iota(jnp.int32, (TOK, TOK), 1)
    own_copy.wait()
    prev_copy.wait()
    for m in range(MB):
        own_row = jnp.broadcast_to(own_ids[m : m + 1, :], (TOK, TOK)).astype(jnp.float32)
        prev_row = jnp.broadcast_to(prev_ids[m : m + 1, :], (TOK, TOK)).astype(jnp.float32)
        prev_row = jnp.where(first_shard, -1.0, prev_row)
        seen = jnp.where(col <= row, own_row, prev_row)
        bias[m] = jnp.where(seen == own_row.T, 0.0, -1e30)

    def halo(slot, which):
        dst = (kcat, vcat)[which]
        return pltpu.make_async_remote_copy(
            src_ref=dst.at[slot, pl.ds(TOK, TOK)],
            dst_ref=dst.at[slot, pl.ds(0, TOK)],
            send_sem=halo_send.at[2 * slot + which],
            recv_sem=halo_recv.at[2 * slot + which],
            device_id=(x, jnp.minimum(c + 1, shards_n - 1)),
            device_id_type=MESH,
        )

    for slot in range(SLOTS):
        for which, dst in enumerate((kcat, vcat)):
            wait_for(dst.at[slot, pl.ds(TOK, TOK)], kv_recv.at[2 * slot + which])

        @pl.when(jnp.logical_not(last_shard))
        def _():
            for which in range(2):
                halo(slot, which).start()

    @pl.when(jnp.logical_not(first_shard))
    def _():
        for slot in range(SLOTS):
            for which, dst in enumerate((kcat, vcat)):
                wait_for(dst.at[slot, pl.ds(0, TOK)], halo_recv.at[2 * slot + which])

    def tri():
        rows = lax.broadcasted_iota(jnp.int32, (ROWS, TOK), 0)
        cols = lax.broadcasted_iota(jnp.int32, (ROWS, TOK), 1)
        return cols <= lax.rem(rows, TOK)

    def split(weights):
        own = tri()
        prev_half = jnp.where(own, 0.0, weights).astype(jnp.bfloat16)
        own_half = jnp.where(own, weights, 0.0).astype(jnp.bfloat16)
        return jnp.concatenate([prev_half, own_half], axis=1)

    def merge(wide):
        return jnp.where(tri(), wide[:, TOK:], wide[:, :TOK])

    def deliver(buf, dst, code, index, kind, remote, local):
        group, layer = field(code, 0), field(code, 1)
        slot, u = index // NU, lax.rem(index, NU)
        src, dst = buf.at[slot, u], columns(dst, group, u)

        @pl.when(layer != x)
        def _():
            remote(move(src, dst, home_send.at[kind, index], home_recv.at[kind], layer))

        if local is not None:

            @pl.when(layer == x)
            def _():
                local(pltpu.make_async_copy(src, dst, home_recv.at[kind]))

    def pass_on(buf, dst, send, recv, code, index, forward, act):
        layer = field(code, 1)
        section, slot = (field(code, 2), field(code, 3)) if forward else (field(code, 4), field(code, 5))
        more = layer < LAYERS - 1 if forward else layer > 0
        own_slot, u = index // NU, lax.rem(index, NU)

        @pl.when(jnp.logical_and(more, section != x))
        def _():
            act(
                move(
                    buf.at[own_slot, u], dst.at[slot, u], send.at[index], recv.at[slot * NU + u], section
                )
            )

    start = lambda copy: copy.start()
    wait_send = lambda copy: copy.wait_send()

    def task_code(t):
        word = choose(t // PER_WORD, words)
        return lax.rem(lax.shift_right_logical(word, 5 * lax.rem(t, PER_WORD)), 32)

    def forward_task(slot, u, code):
        index = slot * NU + u
        layer = field(code, 1)
        wait_for(qbuf.at[slot, u], q_recv.at[index])

        @pl.when(jnp.logical_and(layer > 0, field(code, 4) != x))
        def _():
            wait_for(fin.at[slot, u], f_recv.at[index])

        carried = stack_heads(fin[slot, u]).astype(jnp.float32)
        carried = jnp.where(layer == 0, 0.0, carried)
        mixed = (stack_heads(qbuf[slot, u]).astype(jnp.float32) + carried).astype(jnp.bfloat16)
        scores = merge(dot(mixed, kcat[slot], NT))
        mask = bias[field(code, 0) // KVH]
        scores = scores + jnp.concatenate([mask] * G, axis=0)
        lifted = jnp.exp2((scores - jnp.max(scores, axis=1, keepdims=True)) * EXP2_SCALE)
        weights = lifted * (1.0 / jnp.sum(lifted, axis=1, keepdims=True))
        wide = split(weights)
        out = side_by_side(dot(wide, vcat[slot], NN).astype(jnp.bfloat16))
        mixbuf[slot, u], wbuf[slot, u], pbuf[slot, u], obuf[slot, u] = mixed, weights, wide, out
        pass_on(obuf, fin, f_send, f_recv, code, index, True, start)
        deliver(obuf, att_hbm, code, index, 0, start, start)

        @pl.when(jnp.logical_and(layer < LAYERS - 1, field(code, 2) == x))
        def _():
            fin[field(code, 3), u] = out

    def backward_task(slot, u, code):
        index = slot * NU + u
        layer = field(code, 1)

        @pl.when(jnp.logical_or(layer == LAYERS - 1, field(code, 2) != x))
        def _():
            wait_for(gin.at[slot, u], b_recv.at[index])

        grad = stack_heads(gin[slot, u])
        weights = wbuf[slot, u]
        weight_grad = merge(dot(grad, vcat[slot], NT))
        row_dot = jnp.sum(weights * weight_grad, axis=1, keepdims=True)
        wide = split(weights * (weight_grad - row_dot) * SCALE)
        out = side_by_side(dot(wide, kcat[slot], NN).astype(jnp.bfloat16))
        dqbuf[slot, u] = out
        pass_on(dqbuf, gin, b_send, b_recv, code, index, False, start)
        deliver(dqbuf, qg_hbm, code, index, 1, start, start)

        @pl.when(jnp.logical_and(layer > 0, field(code, 4) == x))
        def _():
            gin[field(code, 5), u] = out

        dkt[slot] += dot(mixbuf[slot, u], wide, TN)
        dvt[slot] += dot(grad, pbuf[slot, u], TN)

        @pl.when(jnp.logical_and(u == NU - 1, jnp.logical_not(first_shard)))
        def _():
            part_send[slot, 0] = dkt[slot, :, :TOK].astype(jnp.bfloat16)
            part_send[slot, 1] = dvt[slot, :, :TOK].astype(jnp.bfloat16)
            part_copy(slot).start()

    def part_copy(slot):
        return pltpu.make_async_remote_copy(
            src_ref=part_send.at[slot],
            dst_ref=part_recv.at[slot],
            send_sem=part_send_sem.at[slot],
            recv_sem=part_recv_sem.at[slot],
            device_id=(x, jnp.maximum(c - 1, 0)),
            device_id_type=MESH,
        )

    @pl.loop(0, STEPS)
    def _(t):
        task = task_code(t)
        slot, u = lax.rem(task // 4, SLOTS), lax.rem(task, 4)
        code = choose(slot, codes)

        @pl.when(task < 16)
        def _():
            forward_task(slot, u, code)

        @pl.when(task >= 16)
        def _():
            backward_task(slot, u, code)

    def kv_deliver(slot, which, act, local):
        group, layer = field(codes[slot], 0), field(codes[slot], 1)
        src, dst = kvout.at[slot, which], kv_columns((kg_hbm, vg_hbm)[which], group)

        @pl.when(layer != x)
        def _():
            act(move(src, dst, home_send.at[2 + which, slot], home_recv.at[2 + which], layer))

        if local is not None:

            @pl.when(layer == x)
            def _():
                local(pltpu.make_async_copy(src, dst, home_recv.at[2 + which]))

    @pl.loop(0, SLOTS)
    def _(i):
        slot = choose(i, [choose(x, [last_slots(s)[j] for s in range(LAYERS)]) for j in range(SLOTS)])

        @pl.when(jnp.logical_not(last_shard))
        def _():
            wait_for(part_recv.at[slot], part_recv_sem.at[slot])

        for which, acc in enumerate((dkt, dvt)):
            extra = jnp.where(last_shard, 0.0, part_recv[slot, which].astype(jnp.float32))
            kvout[slot, which] = (acc[slot, :, TOK:] + extra).T.astype(jnp.bfloat16)
        code = choose(slot, codes)
        group, layer = field(code, 0), field(code, 1)
        for which, dst in enumerate((kg_hbm, vg_hbm)):
            src, dst = kvout.at[slot, which], kv_columns(dst, group)

            @pl.when(layer != x)
            def _():
                move(src, dst, home_send.at[2 + which, slot], home_recv.at[2 + which], layer).start()

            @pl.when(layer == x)
            def _():
                pltpu.make_async_copy(src, dst, home_recv.at[2 + which]).start()

    for g in range(NGRP):

        @pl.when(places[g][0] != x)
        def _():
            for which in range(2):
                kv_move(g, which).wait_send()
            for u in range(NU):
                q_move(g, u).wait_send()

    for slot in range(SLOTS):

        @pl.when(jnp.logical_not(last_shard))
        def _():
            for which in range(2):
                halo(slot, which).wait_send()

        @pl.when(jnp.logical_not(first_shard))
        def _():
            part_copy(slot).wait_send()

        for u in range(NU):
            index = slot * NU + u
            pass_on(obuf, fin, f_send, f_recv, codes[slot], index, True, wait_send)
            pass_on(dqbuf, gin, b_send, b_recv, codes[slot], index, False, wait_send)
            deliver(obuf, att_hbm, codes[slot], index, 0, wait_send, None)
            deliver(dqbuf, qg_hbm, codes[slot], index, 1, wait_send, None)
        for which in range(2):
            kv_deliver(slot, which, wait_send, None)
    for kind, dst in enumerate((att_hbm, qg_hbm, kg_hbm, vg_hbm)):
        wait_for(dst, home_recv.at[kind])


def last_slots(section):
    ends = {}
    for t, task in enumerate(ORDER[section]):
        if task >= 16:
            ends[task // 4 % SLOTS] = t
    return sorted(ends, key=ends.get)


def shards(query_in, key_in, value_in, doc_ids, out_grad):
    shards_n = lax.axis_size("ctx")
    bf16, f32 = jnp.bfloat16, jnp.float32
    feat, kv = HEADS * HD, KVH * HD
    hbm = pl.BlockSpec(memory_space=pl.ANY)
    dma = pltpu.SemaphoreType.DMA
    att, qg, kg, vg = pl.pallas_call(
        functools.partial(kernel, shards_n),
        out_shape=(
            jax.ShapeDtypeStruct((MB, TOK, feat), bf16),
            jax.ShapeDtypeStruct((MB, TOK, feat), bf16),
            jax.ShapeDtypeStruct((MB, TOK, kv), bf16),
            jax.ShapeDtypeStruct((MB, TOK, kv), bf16),
        ),
        in_specs=[hbm] * 5,
        out_specs=[hbm] * 4,
        scratch_shapes=[
            pltpu.VMEM((SLOTS, NU, TOK, COLS), bf16),
            pltpu.VMEM((SLOTS, NU, TOK, COLS), bf16),
            pltpu.VMEM((SLOTS, NU, TOK, COLS), bf16),
            pltpu.VMEM((SLOTS, NU, TOK, COLS), bf16),
            pltpu.VMEM((SLOTS, NU, TOK, COLS), bf16),
            pltpu.VMEM((SLOTS, NU, ROWS, HD), bf16),
            pltpu.VMEM((SLOTS, NU, ROWS, TOK), f32),
            pltpu.VMEM((SLOTS, NU, ROWS, 2 * TOK), bf16),
            pltpu.VMEM((SLOTS, 2 * TOK, HD), bf16),
            pltpu.VMEM((SLOTS, 2 * TOK, HD), bf16),
            pltpu.VMEM((MB, TOK, TOK), f32),
            pltpu.VMEM((MB, TOK), jnp.int32),
            pltpu.VMEM((MB, TOK), jnp.int32),
            pltpu.VMEM((SLOTS, HD, 2 * TOK), f32),
            pltpu.VMEM((SLOTS, HD, 2 * TOK), f32),
            pltpu.VMEM((SLOTS, 2, HD, TOK), bf16),
            pltpu.VMEM((SLOTS, 2, HD, TOK), bf16),
            pltpu.VMEM((SLOTS, 2, TOK, HD), bf16),
            dma((2,)),
            dma((NGRP * NU,)),
            dma((SLOTS * NU,)),
            dma((2 * NGRP,)),
            dma((2 * SLOTS,)),
            dma((2 * SLOTS,)),
            dma((2 * SLOTS,)),
            dma((SLOTS * NU,)),
            dma((SLOTS * NU,)),
            dma((SLOTS * NU,)),
            dma((SLOTS * NU,)),
            dma((SLOTS,)),
            dma((SLOTS,)),
            dma((4, SLOTS * NU)),
            dma((4,)),
        ],
        compiler_params=pltpu.CompilerParams(
            collective_id=0, has_side_effects=True, vmem_limit_bytes=60 * 1024 * 1024
        ),
        cost_estimate=pl.CostEstimate(flops=2_000_000_000, bytes_accessed=5_000_000, transcendentals=600_000),
    )(query_in[0], key_in[0], value_in[0], doc_ids, out_grad)
    return (att[None], qg[None], kg[None], vg[None])


def solution(mesh):
    split = P("section", None, "ctx", None)
    return jax.shard_map(
        shards,
        mesh=mesh,
        in_specs=(split, split, split, P(), P(None, "ctx", None)),
        out_specs=(split, split, split, split),
        check_vma=False,
    )
```

time: 86.8 us -> 53.9 us (0.62)
  Pallas kernels: 77.5 us -> 47.5 us
  local copies, waits for them, and re-layouts: 8.4 us -> 5.02 us
    pallas_call x1, Pallas kernels: 77.5 us -> 47.5 us  [shards(): pl.pallas_call(functools.partial(kernel, shards_n), out_shape=(jax.ShapeD...]
    unnamed x14 -> x10, local copies, waits for them, and re-layouts: 8.4 us -> 5.02 us
where the time goes in v1:
time: 53.9 us; the launch traced here: 53.2 us
  Pallas kernels  47.5 us (88%)
  local copies, waits for them, and re-layouts  5.02 us (9%)
  between operations  0.65 us (1%)
    pallas_call x1, Pallas kernels, shards(): pl.pallas_call(functools.partial(kernel, shards_n), out_shape=(jax.ShapeD...  47.5 us
    unnamed x10, local copies, waits for them, and re-layouts  5.02 us

profile of v1, /device:TPU:56, one launch (start us, length us, event | category | flops | bytes accessed | tf_op | source)
XLA Modules:
  0.0 53.2 jit_solution(11072265479800439136)
XLA Ops:
  0.6 47.5 %shard_map.84 = (bf16[2,128,2048]{2,1,0:T(8,128)(2,1)}, bf16[2,128,2048]{2,1,0:T(8,128)(2,1)}, bf16[2,128,256]{2,1,0:T(8,128)(2,1)}, bf16[2,128,256]{2,1,0:T(8,128)(2,1)}) custom-call(bf16[2,128,2048]{2,1,0:T(8,128)(2,1)} %bitcast.11, bf16[2,128,256]{2,1,0:T(8,128)(2,1)} %bitcast.12, bf16[2,128,256]{2,1,0:T(8,128)(2,1)} %bitcast.13, s32[2,16384]{1,0:T(2,128)} %ids_hbm.1, ...), custom_call_target="tpu_custom_call" | custom-call | flops 2000000000 | bytes 5000000 | tf_op jit(solution)/shard_map/pallas_call | solution.py:495
  48.1 0.0 copy-start
  48.1 2.4 %copy.13 = bf16[1,2,128,2048]{3,2,1,0:T(8,128)(2,1)} copy(bf16[1,2,128,2048]{3,2,1,0:T(8,128)(2,1)} %bitcast.8) | data formatting | bytes 2097152
  50.5 0.0 copy-done
  50.5 0.0 copy-start.2
  50.5 1.0 %copy.14 = bf16[1,2,128,2048]{3,2,1,0:T(8,128)(2,1)} copy(bf16[1,2,128,2048]{3,2,1,0:T(8,128)(2,1)S(1)} %bitcast.7) | data formatting | bytes 2097152
  51.5 0.1 copy-done.2
  51.5 0.0 copy-start.1
  51.6 0.7 %copy.15 = bf16[1,2,128,256]{3,2,1,0:T(8,128)(2,1)} copy(bf16[1,2,128,256]{3,2,1,0:T(8,128)(2,1)S(1)} %bitcast.10) | data formatting | bytes 262144
  52.2 0.3 copy-done.1
  52.5 0.7 %copy.16 = bf16[1,2,128,256]{3,2,1,0:T(8,128)(2,1)} copy(bf16[1,2,128,256]{3,2,1,0:T(8,128)(2,1)S(1)} %bitcast.9) | data formatting | bytes 262144
Async XLA Ops:
  48.1 2.4 %copy-start = (bf16[2,128,2048]{2,1,0:T(8,128)(2,1)S(1)}, bf16[2,128,2048]{2,1,0:T(8,128)(2,1)}, u32[]{:S(2)}) copy-start(bf16[2,128,2048]{2,1,0:T(8,128)(2,1)} %get-tuple-element.9) | copy-start | bytes 3145732
  50.5 1.0 %copy-start.2 = (bf16[2,128,256]{2,1,0:T(8,128)(2,1)S(1)}, bf16[2,128,256]{2,1,0:T(8,128)(2,1)}, u32[]{:S(2)}) copy-start(bf16[2,128,256]{2,1,0:T(8,128)(2,1)} %get-tuple-element.10) | copy-start | bytes 393220
  51.5 1.0 %copy-start.1 = (bf16[2,128,256]{2,1,0:T(8,128)(2,1)S(1)}, bf16[2,128,256]{2,1,0:T(8,128)(2,1)}, u32[]{:S(2)}) copy-start(bf16[2,128,256]{2,1,0:T(8,128)(2,1)} %get-tuple-element.11) | copy-start | bytes 393220

commit v2 on v1

--- a/solution.py
+++ b/solution.py
@@ -209,7 +209,7 @@
     pl.semaphore_wait(barrier, jnp.where(last_shard, LAYERS - 1, LAYERS))
 
     def kv_move(g, which):
-        section, slot = places[g]
+        section, slot = g, x
         src, dst = ((k_hbm, kcat), (v_hbm, vcat))[which]
         return move(
             kv_columns(src, g),
@@ -220,24 +220,18 @@
         )
 
     def q_move(g, u):
-        section, slot = places[g]
+        section, slot = g, x
         return move(
             columns(q_hbm, g, u), qbuf.at[slot, u], q_send.at[g * NU + u], q_recv.at[slot * NU + u], section
         )
 
-    for g in range(NGRP):
-
-        @pl.when(places[g][0] != x)
-        def _():
-            for which in range(2):
-                kv_move(g, which).start()
-
+    order = [lax.rem(x + d, NGRP) for d in (2, 1, 3)]
+    for g in order:
+        for which in range(2):
+            kv_move(g, which).start()
     for u in range(NU):
-        for g in range(NGRP):
-
-            @pl.when(places[g][0] != x)
-            def _():
-                q_move(g, u).start()
+        for g in order:
+            q_move(g, u).start()
 
     row = lax.broadcasted_iota(jnp.int32, (TOK, TOK), 0)
     col = lax.broadcasted_iota(jnp.int32, (TOK, TOK), 1)
@@ -446,14 +440,11 @@
             def _():
                 pltpu.make_async_copy(src, dst, home_recv.at[2 + which]).start()
 
-    for g in range(NGRP):
-
-        @pl.when(places[g][0] != x)
-        def _():
-            for which in range(2):
-                kv_move(g, which).wait_send()
-            for u in range(NU):
-                q_move(g, u).wait_send()
+    for g in order:
+        for which in range(2):
+            kv_move(g, which).wait_send()
+        for u in range(NU):
+            q_move(g, u).wait_send()
 
     for slot in range(SLOTS):
 
@@ -486,6 +477,14 @@
     return sorted(ends, key=ends.get)
 
 
+def settle(*refs):
+    copies = [pltpu.make_async_copy(refs[i], refs[4 + i], refs[8].at[i]) for i in range(4)]
+    for copy in copies:
+        copy.start()
+    for copy in copies:
+        copy.wait()
+
+
 def shards(query_in, key_in, value_in, doc_ids, out_grad):
     shards_n = lax.axis_size("ctx")
     bf16, f32 = jnp.bfloat16, jnp.float32
@@ -495,13 +494,13 @@
     att, qg, kg, vg = pl.pallas_call(
         functools.partial(kernel, shards_n),
         out_shape=(
-            jax.ShapeDtypeStruct((MB, TOK, feat), bf16),
-            jax.ShapeDtypeStruct((MB, TOK, feat), bf16),
-            jax.ShapeDtypeStruct((MB, TOK, kv), bf16),
-            jax.ShapeDtypeStruct((MB, TOK, kv), bf16),
+            pltpu.VMEM((MB, TOK, feat), bf16),
+            pltpu.VMEM((MB, TOK, feat), bf16),
+            pltpu.VMEM((MB, TOK, kv), bf16),
+            pltpu.VMEM((MB, TOK, kv), bf16),
         ),
         in_specs=[hbm] * 5,
-        out_specs=[hbm] * 4,
+        out_specs=[pl.BlockSpec(memory_space=pltpu.VMEM)] * 4,
         scratch_shapes=[
             pltpu.VMEM((SLOTS, NU, TOK, COLS), bf16),
             pltpu.VMEM((SLOTS, NU, TOK, COLS), bf16),
@@ -538,10 +537,18 @@
             dma((4,)),
         ],
         compiler_params=pltpu.CompilerParams(
-            collective_id=0, has_side_effects=True, vmem_limit_bytes=60 * 1024 * 1024
+            collective_id=0, has_side_effects=True, vmem_limit_bytes=32 * 1024 * 1024
         ),
         cost_estimate=pl.CostEstimate(flops=2_000_000_000, bytes_accessed=5_000_000, transcendentals=600_000),
-    )(query_in[0], key_in[0], value_in[0], doc_ids, out_grad)
+    )(*[pltpu.with_memory_space_constraint(a, pltpu.HBM) for a in (query_in[0], key_in[0], value_in[0], doc_ids, out_grad)])
+    att, qg, kg, vg = pl.pallas_call(
+        settle,
+        out_shape=[jax.ShapeDtypeStruct(a.shape, a.dtype) for a in (att, qg, kg, vg)],
+        in_specs=[hbm] * 4,
+        out_specs=[hbm] * 4,
+        scratch_shapes=[dma((4,))],
+        compiler_params=pltpu.CompilerParams(vmem_limit_bytes=1 * 1024 * 1024),
+    )(att, qg, kg, vg)
     return (att[None], qg[None], kg[None], vg[None])
 
 

time: 53.9 us -> 49.6 us (0.920); the launches traced: 53.2 us -> 49.4 us
  local copies, waits for them, and re-layouts: 5.02 us -> 0 us
  Pallas kernels: 47.5 us -> 48.8 us
    unnamed x10 -> x0, local copies, waits for them, and re-layouts: 5.02 us -> none
    pallas_call x1 -> x2, Pallas kernels: 47.5 us -> 48.8 us  [the longest x1 47.4 us: shards(): pl.pallas_call(functools.partial(kernel, shards_n), out_shape=(pltpu.VMEM...]
where the time goes in v2:
time: 49.6 us; the launch traced here: 49.4 us
  Pallas kernels  48.8 us (98%)
  between operations  0.64 us (1%)
    pallas_call x1, Pallas kernels, shards(): pl.pallas_call(functools.partial(kernel, shards_n), out_shape=(pltpu.VMEM...  47.4 us
    pallas_call x1, Pallas kernels, shards(): pl.pallas_call(settle, out_shape=[jax.ShapeDtypeStruct(a.shape, a.dtype)...  1.43 us

profile of v2, /device:TPU:56, one launch (start us, length us, event | category | flops | bytes accessed | tf_op | source)
XLA Modules:
  0.0 49.4 jit_solution(6608685557325644963)
XLA Ops:
  0.6 47.4 %shard_map.84 = (bf16[2,128,2048]{2,1,0:T(8,128)(2,1)S(1)}, bf16[2,128,2048]{2,1,0:T(8,128)(2,1)S(1)}, bf16[2,128,256]{2,1,0:T(8,128)(2,1)S(1)}, bf16[2,128,256]{2,1,0:T(8,128)(2,1)S(1)}) custom-call(bf16[2,128,2048]{2,1,0:T(8,128)(2,1)} %bitcast.7, bf16[2,128,256]{2,1,0:T(8,128)(2,1)} %bitcast.10, bf16[2,128,256]{2,1,0:T(8,128)(2,1)} %bitcast.11, ...), custom_call_target="tpu_custom_call" | custom-call | flops 2000000000 | bytes 5000000 | tf_op jit(solution)/shard_map/pallas_call | solution.py:494
  48.0 1.4 %shard_map.85 = (bf16[2,128,2048]{2,1,0:T(8,128)(2,1)}, bf16[2,128,2048]{2,1,0:T(8,128)(2,1)}, bf16[2,128,256]{2,1,0:T(8,128)(2,1)}, bf16[2,128,256]{2,1,0:T(8,128)(2,1)}) custom-call(bf16[2,128,2048]{2,1,0:T(8,128)(2,1)S(1)} %get-tuple-element.12.refs_0_, bf16[2,128,2048]{2,1,0:T(8,128)(2,1)S(1)} %get-tuple-element.13.refs_1_, ...), custom_call_target="tpu_custom_call" | custom-call | tf_op jit(solution)/shard_map/pallas_call | solution.py:544

commit v3 on v2

v3 whole, which is shorter than its diff:
```python
import functools
import math

import jax
import jax.numpy as jnp
from jax import lax
from jax.experimental import pallas as pl
from jax.experimental.pallas import tpu as pltpu
from jax.sharding import PartitionSpec as P

HD = 128
GROUP = 8
KVH = 2
HEADS = GROUP * KVH
MB = 2
TOK = 128
LAYERS = 4
DIRECT = 1
ROW = 16
FAR = LAYERS
SLOTS = LAYERS + 1
NGRP = MB * KVH
G = 4
NU = GROUP // G
COLS = G * HD
ROWS = G * TOK
MESH = pl.DeviceIdType.MESH
SCALE = 1.0 / math.sqrt(HD)
EXP2_SCALE = math.log2(math.e) / math.sqrt(HD)
NT = (((1,), (1,)), ((), ()))
NN = (((1,), (0,)), ((), ()))
TN = (((0,), (0,)), ((), ()))

def dot(a, b, dims):
    return lax.dot_general(a, b, dims, preferred_element_type=jnp.float32)


def stack_heads(x):
    return jnp.concatenate([x[:, h * HD : (h + 1) * HD] for h in range(G)], axis=0)


def side_by_side(x):
    return jnp.concatenate([x[h * TOK : (h + 1) * TOK] for h in range(G)], axis=1)


def kernel(
    shards_n,
    q_hbm,
    k_hbm,
    v_hbm,
    ids_hbm,
    og_hbm,
    att_hbm,
    qg_hbm,
    kg_hbm,
    vg_hbm,
    qbuf,
    gin,
    far_in,
    obuf,
    dqbuf,
    mixbuf,
    wbuf,
    pbuf,
    kcat,
    vcat,
    bias,
    own_ids,
    prev_ids,
    dkt,
    dvt,
    part_send,
    part_recv,
    kvout,
    ids_sem,
    q_send,
    q_recv,
    kv_send,
    kv_recv,
    halo_send,
    halo_recv,
    b_recv,
    part_send_sem,
    part_recv_sem,
    home_send,
    home_recv,
    near_send,
    near_recv,
    far_send,
    far_recv,
    direct_send,
):
    x = lax.axis_index("section")
    c = lax.axis_index("ctx")
    first_shard = c == 0
    last_shard = c == shards_n - 1
    edge = jnp.logical_and(lax.rem(c, ROW) == ROW - 1, jnp.logical_not(last_shard))
    after_edge = jnp.logical_and(lax.rem(c, ROW) == 0, jnp.logical_not(first_shard))
    after, before, opposite = (lax.rem(x + d, LAYERS) for d in (1, 3, 2))

    barrier = pltpu.get_barrier_semaphore()
    for d in range(1, LAYERS):
        pl.semaphore_signal(barrier, inc=1, device_id=(lax.rem(x + d, LAYERS), c), device_id_type=MESH)

    @pl.when(jnp.logical_not(first_shard))
    def _():
        pl.semaphore_signal(barrier, inc=1, device_id=(x, jnp.maximum(c - 1, 0)), device_id_type=MESH)

    @pl.when(after_edge)
    def _():
        for section in (after, before, opposite):
            pl.semaphore_signal(
                barrier, inc=1, device_id=(section, jnp.maximum(c - 1, 0)), device_id_type=MESH
            )

    def move(src, dst, send_sem, recv_sem, section):
        return pltpu.make_async_remote_copy(
            src_ref=src,
            dst_ref=dst,
            send_sem=send_sem,
            recv_sem=recv_sem,
            device_id=(section, c),
            device_id_type=MESH,
        )

    def wait_for(ref, sem):
        pltpu.make_async_copy(ref, ref, sem).wait()

    def columns(ref, group, unit):
        m, n = group // KVH, lax.rem(group, KVH)
        return ref.at[m, :, pl.ds(pl.multiple_of(n * GROUP * HD + unit * COLS, COLS), COLS)]

    def kv_columns(ref, group):
        m, n = group // KVH, lax.rem(group, KVH)
        return ref.at[m, :, pl.ds(pl.multiple_of(n * HD, HD), HD)]

    own_at = pl.multiple_of(c * TOK, TOK)
    prev_at = pl.multiple_of(jnp.maximum(c - 1, 0) * TOK, TOK)
    own_copy = pltpu.make_async_copy(ids_hbm.at[:, pl.ds(own_at, TOK)], own_ids, ids_sem.at[0])
    prev_copy = pltpu.make_async_copy(ids_hbm.at[:, pl.ds(prev_at, TOK)], prev_ids, ids_sem.at[1])
    own_copy.start()
    prev_copy.start()

    for which, (src, dst) in enumerate(((k_hbm, kcat), (v_hbm, vcat))):
        pltpu.make_async_copy(kv_columns(src, x), dst.at[x, pl.ds(TOK, TOK)], kv_recv.at[2 * x + which]).start()
        pltpu.make_async_copy(
            kv_columns(src, opposite), dst.at[FAR, pl.ds(TOK, TOK)], kv_recv.at[2 * FAR + which]
        ).start()
    for u in range(NU):
        pltpu.make_async_copy(columns(q_hbm, x, u), qbuf.at[x, u], q_recv.at[x * NU + u]).start()
        pltpu.make_async_copy(columns(q_hbm, opposite, u), qbuf.at[FAR, u], q_recv.at[FAR * NU + u]).start()
        pltpu.make_async_copy(columns(og_hbm, x, u), gin.at[u], b_recv.at[u]).start()

        @pl.when(x == LAYERS - 1)
        def _():
            pltpu.make_async_copy(columns(og_hbm, opposite, u), far_in.at[1, u], far_recv.at[1, u]).start()

    dkt[...] = jnp.zeros_like(dkt)
    dvt[...] = jnp.zeros_like(dvt)

    @pl.when(first_shard)
    def _():
        for slot in range(SLOTS):
            kcat[slot, :TOK] = jnp.zeros((TOK, HD), jnp.bfloat16)
            vcat[slot, :TOK] = jnp.zeros((TOK, HD), jnp.bfloat16)

    heard = jnp.where(last_shard, LAYERS - 1, jnp.where(edge, 2 * LAYERS - 1, LAYERS))
    pl.semaphore_wait(barrier, heard)

    others = (opposite, after, before)

    def kv_move(g, which):
        src, dst = ((k_hbm, kcat), (v_hbm, vcat))[which]
        return move(
            kv_columns(src, g),
            dst.at[x, pl.ds(TOK, TOK)],
            kv_send.at[2 * g + which],
            kv_recv.at[2 * x + which],
            g,
        )

    def q_move(g, u):
        return move(columns(q_hbm, g, u), qbuf.at[x, u], q_send.at[g * NU + u], q_recv.at[x * NU + u], g)

    def edge_move(g, which):
        src, dst = ((k_hbm, kcat), (v_hbm, vcat))[which]
        return pltpu.make_async_remote_copy(
            src_ref=kv_columns(src, g),
            dst_ref=dst.at[x, pl.ds(0, TOK)],
            send_sem=halo_send.at[2 * g + which],
            recv_sem=halo_recv.at[2 * x + which],
            device_id=(g, jnp.minimum(c + 1, shards_n - 1)),
            device_id_type=MESH,
        )

    @pl.when(edge)
    def _():
        for g in others:
            for which in range(2):
                edge_move(g, which).start()

    for g in others:
        for which in range(2):
            kv_move(g, which).start()
    for u in range(NU):
        for g in others:
            q_move(g, u).start()

    row = lax.broadcasted_iota(jnp.int32, (TOK, TOK), 0)
    col = lax.broadcasted_iota(jnp.int32, (TOK, TOK), 1)
    own_copy.wait()
    prev_copy.wait()
    for m in range(MB):
        own_row = jnp.broadcast_to(own_ids[m : m + 1, :], (TOK, TOK)).astype(jnp.float32)
        prev_row = jnp.broadcast_to(prev_ids[m : m + 1, :], (TOK, TOK)).astype(jnp.float32)
        prev_row = jnp.where(first_shard, -1.0, prev_row)
        seen = jnp.where(col <= row, own_row, prev_row)
        bias[m] = jnp.where(seen == own_row.T, 0.0, -1e30)

    def hands_on(slot):
        if slot == FAR:
            return True
        return jnp.logical_or(jnp.logical_not(edge), slot == x)

    def halo(slot, which):
        dst = (kcat, vcat)[which]
        return pltpu.make_async_remote_copy(
            src_ref=dst.at[slot, pl.ds(TOK, TOK)],
            dst_ref=dst.at[slot, pl.ds(0, TOK)],
            send_sem=halo_send.at[2 * slot + which],
            recv_sem=halo_recv.at[2 * slot + which],
            device_id=(x, jnp.minimum(c + 1, shards_n - 1)),
            device_id_type=MESH,
        )

    for slot in (FAR, *range(LAYERS)):
        for which, dst in enumerate((kcat, vcat)):
            wait_for(dst.at[slot, pl.ds(TOK, TOK)], kv_recv.at[2 * slot + which])

        @pl.when(jnp.logical_and(jnp.logical_not(last_shard), hands_on(slot)))
        def _():
            for which in range(2):
                halo(slot, which).start()

    def tri():
        rows = lax.broadcasted_iota(jnp.int32, (ROWS, TOK), 0)
        cols = lax.broadcasted_iota(jnp.int32, (ROWS, TOK), 1)
        return cols <= lax.rem(rows, TOK)

    def split(weights):
        own = tri()
        prev_half = jnp.where(own, 0.0, weights).astype(jnp.bfloat16)
        own_half = jnp.where(own, weights, 0.0).astype(jnp.bfloat16)
        return jnp.concatenate([prev_half, own_half], axis=1)

    def merge(wide):
        return jnp.where(tri(), wide[:, TOK:], wide[:, :TOK])

    results = ((obuf, att_hbm), (dqbuf, qg_hbm))

    def home_move(kind, u):
        buf, dst = results[kind]
        layer = (before, after)[kind]
        return move(buf.at[layer, u], columns(dst, x, u), home_send.at[kind, u], home_recv.at[kind], layer)

    def near_move(kind, u):
        buf, dst = results[kind]
        layer = (after, before)[kind]
        return move(buf.at[layer, u], columns(dst, x, u), near_send.at[kind, u], near_recv.at[kind, u], layer)

    def far_move(kind, u):
        dst = results[kind][1]
        group, section = ((before, after), (after, before))[kind]
        return move(
            columns(dst, group, u), far_in.at[kind, u], far_send.at[kind, u], far_recv.at[kind, u], section
        )

    def direct_move(u):
        return move(
            dqbuf.at[before, u], far_in.at[1, u], direct_send.at[u], far_recv.at[1, u], opposite
        )

    more = (x < LAYERS - 1, x > 0)

    def pass_on(kind, u):
        group = (before, after)[kind]
        wait_for(columns(results[kind][1], group, u), near_recv.at[kind, u])

        @pl.when(jnp.logical_and(more[kind], u < (NU, DIRECT)[kind]))
        def _():
            far_move(kind, u).start()

    def keep(kind, slot, group, u):
        buf, dst = results[kind]
        pltpu.make_async_copy(buf.at[slot, u], columns(dst, group, u), home_recv.at[kind]).start()

    def forward_task(slot, u, group, carried):
        wait_for(qbuf.at[slot, u], q_recv.at[slot * NU + u])

        @pl.when(jnp.logical_and(u == 0, jnp.logical_not(first_shard)))
        def _():
            for which, dst in enumerate((kcat, vcat)):
                wait_for(dst.at[slot, pl.ds(0, TOK)], halo_recv.at[2 * slot + which])

        mixed = (stack_heads(qbuf[slot, u]).astype(jnp.float32) + carried).astype(jnp.bfloat16)
        scores = merge(dot(mixed, kcat[slot], NT))
        mask = bias[group // KVH]
        scores = scores + jnp.concatenate([mask] * G, axis=0)
        lifted = jnp.exp2((scores - jnp.max(scores, axis=1, keepdims=True)) * EXP2_SCALE)
        weights = lifted * (1.0 / jnp.sum(lifted, axis=1, keepdims=True))
        wide = split(weights)
        out = side_by_side(dot(wide, vcat[slot], NN).astype(jnp.bfloat16))
        mixbuf[slot, u], wbuf[slot, u], pbuf[slot, u], obuf[slot, u] = mixed, weights, wide, out

    def backward_task(slot, u, grad, sums):
        grad = stack_heads(grad)
        weights = wbuf[slot, u]
        weight_grad = merge(dot(grad, vcat[slot], NT))
        row_dot = jnp.sum(weights * weight_grad, axis=1, keepdims=True)
        wide = split(weights * (weight_grad - row_dot) * SCALE)
        dqbuf[slot, u] = side_by_side(dot(wide, kcat[slot], NN).astype(jnp.bfloat16))

        @pl.when(sums)
        def _():
            dkt[slot] += dot(mixbuf[slot, u], wide, TN)
            dvt[slot] += dot(grad, pbuf[slot, u], TN)

            @pl.when(jnp.logical_and(u == NU - 1, jnp.logical_not(first_shard)))
            def _():
                part_send[slot, 0] = dkt[slot, :, :TOK].astype(jnp.bfloat16)
                part_send[slot, 1] = dvt[slot, :, :TOK].astype(jnp.bfloat16)
                part_copy(slot).start()

    def part_copy(slot):
        return pltpu.make_async_remote_copy(
            src_ref=part_send.at[slot],
            dst_ref=part_recv.at[slot],
            send_sem=part_send_sem.at[slot],
            recv_sem=part_recv_sem.at[slot],
            device_id=(x, jnp.maximum(c - 1, 0)),
            device_id_type=MESH,
        )

    def forward_own(u):
        @pl.loop(0, LAYERS)
        def _(layer):
            carried = stack_heads(obuf[jnp.maximum(layer - 1, 0), u]).astype(jnp.float32)
            forward_task(layer, u, x, jnp.where(layer == 0, 0.0, carried))

            @pl.when(layer == after)
            def _():
                near_move(0, u).start()

        keep(0, x, x, u)

    def backward_own(u):
        @pl.loop(0, LAYERS)
        def _(i):
            layer = LAYERS - 1 - i
            below = dqbuf[jnp.minimum(layer + 1, LAYERS - 1), u]
            backward_task(layer, u, jnp.where(layer == LAYERS - 1, gin[u], below), layer != opposite)

            @pl.when(layer == before)
            def _():
                near_move(1, u).start()

                @pl.when(jnp.logical_and(u >= DIRECT, opposite < LAYERS - 1))
                def _():
                    direct_move(u).start()

        keep(1, x, x, u)

    def kv_sums(slot):
        @pl.when(jnp.logical_not(last_shard))
        def _():
            wait_for(part_recv.at[slot], part_recv_sem.at[slot])

        for which, acc in enumerate((dkt, dvt)):
            extra = jnp.where(last_shard, 0.0, part_recv[slot, which].astype(jnp.float32))
            kvout[slot, which] = (acc[slot, :, TOK:] + extra).T.astype(jnp.bfloat16)

    def kv_home(layer, which):
        return move(
            kvout.at[layer, which],
            kv_columns((kg_hbm, vg_hbm)[which], x),
            home_send.at[2 + which, layer],
            home_recv.at[2 + which],
            layer,
        )

    def kv_keep(slot, group):
        for which, dst in enumerate((kg_hbm, vg_hbm)):
            pltpu.make_async_copy(kvout.at[slot, which], kv_columns(dst, group), home_recv.at[2 + which]).start()

    def kv_own():
        @pl.loop(0, LAYERS)
        def _(i):
            layer = LAYERS - 1 - i

            @pl.when(layer != opposite)
            def _():
                kv_sums(layer)

                @pl.when(layer != x)
                def _():
                    for which in range(2):
                        kv_home(layer, which).start()

                @pl.when(layer == x)
                def _():
                    kv_keep(layer, x)

    def forward_far(u):
        @pl.when(x > 0)
        def _():
            wait_for(far_in.at[0, u], far_recv.at[0, u])

        carried = stack_heads(far_in[0, u]).astype(jnp.float32)
        forward_task(FAR, u, opposite, jnp.where(x == 0, 0.0, carried))
        keep(0, FAR, opposite, u)

    def backward_far(u):
        wait_for(far_in.at[1, u], far_recv.at[1, u])
        backward_task(FAR, u, far_in[1, u], True)
        keep(1, FAR, opposite, u)

    for u in range(NU):
        wait_for(gin.at[u], b_recv.at[u])

    forward_own(0)
    backward_own(0)
    home_move(0, 0).start()
    forward_own(1)
    pass_on(0, 0)
    backward_own(1)
    pass_on(0, 1)
    home_move(1, 0).start()
    pass_on(1, 0)
    home_move(1, 1).start()
    forward_far(0)
    forward_far(1)
    home_move(0, 1).start()
    backward_far(0)
    kv_own()
    backward_far(1)
    pass_on(1, 1)
    kv_sums(FAR)
    kv_keep(FAR, opposite)

    @pl.when(edge)
    def _():
        for g in others:
            for which in range(2):
                edge_move(g, which).wait_send()

    for other in others:
        for which in range(2):
            kv_move(other, which).wait_send()
        for u in range(NU):
            q_move(other, u).wait_send()
    for other in (after, before):
        for which in range(2):
            kv_home(other, which).wait_send()
    for u in range(NU):
        for kind in range(2):
            home_move(kind, u).wait_send()
            near_move(kind, u).wait_send()

            if kind == 0 or u < DIRECT:

                @pl.when(more[kind])
                def _():
                    far_move(kind, u).wait_send()

        if u >= DIRECT:

            @pl.when(opposite < LAYERS - 1)
            def _():
                direct_move(u).wait_send()

    for slot in range(SLOTS):

        @pl.when(jnp.logical_and(jnp.logical_not(last_shard), hands_on(slot)))
        def _():
            for which in range(2):
                halo(slot, which).wait_send()

        @pl.when(jnp.logical_and(slot != opposite, jnp.logical_not(first_shard)))
        def _():
            part_copy(slot).wait_send()

    kept = pl.ds(0, TOK * (LAYERS - 1) // LAYERS)
    for kind, dst in enumerate((att_hbm, qg_hbm)):
        wait_for(dst.at[:, kept], home_recv.at[kind])
    for which, dst in enumerate((kg_hbm, vg_hbm)):
        wait_for(dst, home_recv.at[2 + which])


def settle(*refs):
    copies = [pltpu.make_async_copy(refs[i], refs[4 + i], refs[8].at[i]) for i in range(4)]
    for copy in copies:
        copy.start()
    for copy in copies:
        copy.wait()


def shards(query_in, key_in, value_in, doc_ids, out_grad):
    shards_n = lax.axis_size("ctx")
    bf16, f32 = jnp.bfloat16, jnp.float32
    feat, kv = HEADS * HD, KVH * HD
    hbm = pl.BlockSpec(memory_space=pl.ANY)
    dma = pltpu.SemaphoreType.DMA
    att, qg, kg, vg = pl.pallas_call(
        functools.partial(kernel, shards_n),
        out_shape=(
            pltpu.VMEM((MB, TOK, feat), bf16),
            pltpu.VMEM((MB, TOK, feat), bf16),
            pltpu.VMEM((MB, TOK, kv), bf16),
            pltpu.VMEM((MB, TOK, kv), bf16),
        ),
        in_specs=[hbm] * 5,
        out_specs=[pl.BlockSpec(memory_space=pltpu.VMEM)] * 4,
        scratch_shapes=[
            pltpu.VMEM((SLOTS, NU, TOK, COLS), bf16),
            pltpu.VMEM((NU, TOK, COLS), bf16),
            pltpu.VMEM((2, NU, TOK, COLS), bf16),
            pltpu.VMEM((SLOTS, NU, TOK, COLS), bf16),
            pltpu.VMEM((SLOTS, NU, TOK, COLS), bf16),
            pltpu.VMEM((SLOTS, NU, ROWS, HD), bf16),
            pltpu.VMEM((SLOTS, NU, ROWS, TOK), f32),
            pltpu.VMEM((SLOTS, NU, ROWS, 2 * TOK), bf16),
            pltpu.VMEM((SLOTS, 2 * TOK, HD), bf16),
            pltpu.VMEM((SLOTS, 2 * TOK, HD), bf16),
            pltpu.VMEM((MB, TOK, TOK), f32),
            pltpu.VMEM((MB, TOK), jnp.int32),
            pltpu.VMEM((MB, TOK), jnp.int32),
            pltpu.VMEM((SLOTS, HD, 2 * TOK), f32),
            pltpu.VMEM((SLOTS, HD, 2 * TOK), f32),
            pltpu.VMEM((SLOTS, 2, HD, TOK), bf16),
            pltpu.VMEM((SLOTS, 2, HD, TOK), bf16),
            pltpu.VMEM((SLOTS, 2, TOK, HD), bf16),
            dma((2,)),
            dma((NGRP * NU,)),
            dma((SLOTS * NU,)),
            dma((2 * NGRP,)),
            dma((2 * SLOTS,)),
            dma((2 * SLOTS,)),
            dma((2 * SLOTS,)),
            dma((NU,)),
            dma((SLOTS,)),
            dma((SLOTS,)),
            dma((4, LAYERS * NU)),
            dma((4,)),
            dma((2, NU)),
            dma((2, NU)),
            dma((2, NU)),
            dma((2, NU)),
            dma((NU,)),
        ],
        compiler_params=pltpu.CompilerParams(
            collective_id=0, has_side_effects=True, vmem_limit_bytes=32 * 1024 * 1024
        ),
        cost_estimate=pl.CostEstimate(flops=2_000_000_000, bytes_accessed=5_000_000, transcendentals=600_000),
    )(*[pltpu.with_memory_space_constraint(a, pltpu.HBM) for a in (query_in[0], key_in[0], value_in[0], doc_ids, out_grad)])
    att, qg, kg, vg = pl.pallas_call(
        settle,
        out_shape=[jax.ShapeDtypeStruct(a.shape, a.dtype) for a in (att, qg, kg, vg)],
        in_specs=[hbm] * 4,
        out_specs=[hbm] * 4,
        scratch_shapes=[dma((4,))],
        compiler_params=pltpu.CompilerParams(vmem_limit_bytes=1 * 1024 * 1024),
    )(att, qg, kg, vg)
    return (att[None], qg[None], kg[None], vg[None])


def solution(mesh):
    split = P("section", None, "ctx", None)
    return jax.shard_map(
        shards,
        mesh=mesh,
        in_specs=(split, split, split, P(), P(None, "ctx", None)),
        out_specs=(split, split, split, split),
        check_vma=False,
    )
```

time: 49.6 us -> 47.8 us (0.964)
  Pallas kernels: 48.8 us -> 47 us
    pallas_call x1, Pallas kernels: 47.4 us -> 45.6 us  [shards(): pl.pallas_call(functools.partial(kernel, shards_n), out_shape=(pltpu.VMEM...]
where the time goes in v3:
time: 47.8 us; the launch traced here: 47.6 us
  Pallas kernels  47 us (98%)
  between operations  0.64 us (1%)
    pallas_call x1, Pallas kernels, shards(): pl.pallas_call(functools.partial(kernel, shards_n), out_shape=(pltpu.VMEM...  45.6 us
    pallas_call x1, Pallas kernels, shards(): pl.pallas_call(settle, out_shape=[jax.ShapeDtypeStruct(a.shape, a.dtype)...  1.43 us

profile of v3, /device:TPU:56, one launch (start us, length us, event | category | flops | bytes accessed | tf_op | source)
XLA Modules:
  0.0 47.6 jit_solution(9263717556527921160)
XLA Ops:
  0.6 45.6 %shard_map.84 = (bf16[2,128,2048]{2,1,0:T(8,128)(2,1)S(1)}, bf16[2,128,2048]{2,1,0:T(8,128)(2,1)S(1)}, bf16[2,128,256]{2,1,0:T(8,128)(2,1)S(1)}, bf16[2,128,256]{2,1,0:T(8,128)(2,1)S(1)}) custom-call(bf16[2,128,2048]{2,1,0:T(8,128)(2,1)} %bitcast.7, bf16[2,128,256]{2,1,0:T(8,128)(2,1)} %bitcast.10, bf16[2,128,256]{2,1,0:T(8,128)(2,1)} %bitcast.11, ...), custom_call_target="tpu_custom_call" | custom-call | flops 2000000000 | bytes 5000000 | tf_op jit(solution)/shard_map/pallas_call | solution.py:513
  46.2 1.4 %shard_map.85 = (bf16[2,128,2048]{2,1,0:T(8,128)(2,1)}, bf16[2,128,2048]{2,1,0:T(8,128)(2,1)}, bf16[2,128,256]{2,1,0:T(8,128)(2,1)}, bf16[2,128,256]{2,1,0:T(8,128)(2,1)}) custom-call(bf16[2,128,2048]{2,1,0:T(8,128)(2,1)S(1)} %get-tuple-element.12.refs_0_, bf16[2,128,2048]{2,1,0:T(8,128)(2,1)S(1)} %get-tuple-element.13.refs_1_, ...), custom_call_target="tpu_custom_call" | custom-call | tf_op jit(solution)/shard_map/pallas_call | solution.py:565

commit v4 on v3

--- a/solution.py
+++ b/solution.py
@@ -438,8 +438,8 @@
     pass_on(1, 0)
     home_move(1, 1).start()
     forward_far(0)
+    home_move(0, 1).start()
     forward_far(1)
-    home_move(0, 1).start()
     backward_far(0)
     kv_own()
     backward_far(1)

time: 47.8 us -> 47.8 us (level)
  no operation moved by 1% of the time
where the time goes in v4:
time: 47.8 us; the launch traced here: 47.6 us
  Pallas kernels  47 us (98%)
  between operations  0.64 us (1%)
    pallas_call x1, Pallas kernels, shards(): pl.pallas_call(functools.partial(kernel, shards_n), out_shape=(pltpu.VMEM...  45.6 us
    pallas_call x1, Pallas kernels, shards(): pl.pallas_call(settle, out_shape=[jax.ShapeDtypeStruct(a.shape, a.dtype)...  1.43 us

profile of v4, /device:TPU:56, one launch (start us, length us, event | category | flops | bytes accessed | tf_op | source)
XLA Modules:
  0.0 47.6 jit_solution(8797517837216797829)
XLA Ops:
  0.6 45.6 %shard_map.84 = (bf16[2,128,2048]{2,1,0:T(8,128)(2,1)S(1)}, bf16[2,128,2048]{2,1,0:T(8,128)(2,1)S(1)}, bf16[2,128,256]{2,1,0:T(8,128)(2,1)S(1)}, bf16[2,128,256]{2,1,0:T(8,128)(2,1)S(1)}) custom-call(bf16[2,128,2048]{2,1,0:T(8,128)(2,1)} %bitcast.7, bf16[2,128,256]{2,1,0:T(8,128)(2,1)} %bitcast.10, bf16[2,128,256]{2,1,0:T(8,128)(2,1)} %bitcast.11, ...), custom_call_target="tpu_custom_call" | custom-call | flops 2000000000 | bytes 5000000 | tf_op jit(solution)/shard_map/pallas_call | solution.py:513
  46.2 1.4 %shard_map.85 = (bf16[2,128,2048]{2,1,0:T(8,128)(2,1)}, bf16[2,128,2048]{2,1,0:T(8,128)(2,1)}, bf16[2,128,256]{2,1,0:T(8,128)(2,1)}, bf16[2,128,256]{2,1,0:T(8,128)(2,1)}) custom-call(bf16[2,128,2048]{2,1,0:T(8,128)(2,1)S(1)} %get-tuple-element.12.refs_0_, bf16[2,128,2048]{2,1,0:T(8,128)(2,1)S(1)} %get-tuple-element.13.refs_1_, ...), custom_call_target="tpu_custom_call" | custom-call | tf_op jit(solution)/shard_map/pallas_call | solution.py:565
